TPU v7x, 256 devices: a whole 4x4x8 slice. The times are simulated.
256 devices in a mesh: grp: 64 (over x, z, y_hi), tp: 4 (over y_lo, core).
Axes of the slice: x: 4, y: 4 (y_hi: 2, y_lo: 2; y = y_hi * 2 + y_lo), z: 8, core: 2. Of those that a mesh axis runs over, the one named last changes fastest.
Arguments:
- queries: bfloat16 [1024, 4096], P('grp', 'tp'), may hold values from -32 to 32
- prefix_kv: bfloat16 [64, 2, 1024, 2048], P('grp', None, None, 'tp'), may hold values from -12 to 12
- suffix_kv: bfloat16 [1024, 2, 32, 2048], P('grp', None, None, 'tp'), may hold values from -6 to 6
- suffix_len: int32 [1024], P('grp'), may hold values from 1 to 32, as said below
- prefill_group: int32 [64], replicated, may hold values from 0 to 63, each once
- sampler_groups: int32 [64, 4], replicated, may hold values from 0 to 63, all different within a row; in each aligned block of 64 rows (0 to 63, 64 to 127, ...) at most 8 rows name the same one
- out_weight: bfloat16 [4096, 4608], P('tp'), may hold values from -1 to 1
- norm_gain: float32 [4608], P('tp'), may hold values from 0.1 to 1.9
- residual: bfloat16 [1024, 4608], P('grp', 'tp'), may hold values from -6 to 6
Outputs:
- mixed: bfloat16 [1024, 4608], P('grp', 'tp')
Inputs may be any that keep to these rules, and one draw needn't show every extreme that they name: `suffix_len`: some sample has all 32 slots live. `prefill_group`: each group prefilled exactly one prompt. `sampler_groups`: a row names 4 different groups; every group is named by 1 to 8 rows, a bound that some block reaches.
All inputs are finite; a program needn't handle non-finite values.
Results may differ from a plain program's by a relative error of at most 0.015.
Values may be sent and summed in bfloat16 or wider, within the bound.
A program may use at most 128 MiB of HBM per device.

v0:
```python
import jax
import jax.numpy as jnp
from jax import lax
from jax.sharding import PartitionSpec as P

D = 4608
HD = 128


score_scale = 144.0 ** (-0.5)
norm_eps = 1e-06


def sample_owners(prefill_group, sampler_groups, per_group):
    prompt_total = prefill_group.shape[0]
    group_ids = jnp.arange(prompt_total, dtype=jnp.int32)
    member = jnp.any(sampler_groups[None, :, :] == group_ids[:, None, None], axis=2).astype(
        jnp.int32
    )
    slot_rank = jnp.cumsum(member, axis=1) - member
    prompt_count = jnp.maximum(jnp.sum(member, axis=1), 1)
    slot_ids = jnp.arange(per_group, dtype=jnp.int32)
    wanted = slot_ids[None, :] % prompt_count[:, None]
    chosen = ((member[:, None, :] == 1) & (slot_rank[:, None, :] == wanted[:, :, None])).astype(
        jnp.int32
    )
    return jnp.sum(chosen * prefill_group[None, None, :], axis=2)


def prefix_partial(query_rows, prefix_keys, prefix_values):
    row_count = query_rows.shape[0]
    key_count = prefix_keys.shape[0]
    kv_count = prefix_keys.shape[1] // HD
    group_size = query_rows.shape[1] // prefix_keys.shape[1]
    query_heads = jnp.transpose(
        query_rows.reshape(row_count, kv_count, group_size, HD), (1, 0, 2, 3)
    )
    key_heads = jnp.transpose(prefix_keys.reshape(key_count, kv_count, HD), (1, 0, 2))
    value_heads = jnp.transpose(prefix_values.reshape(key_count, kv_count, HD), (1, 0, 2))

    def one_head(pieces):
        query_one, key_one, value_one = pieces
        scores = (
            jnp.einsum("rgd,td->rgt", query_one, key_one, preferred_element_type=jnp.float32)
            * score_scale
        )
        row_max = jnp.max(scores, axis=2)
        weights = jnp.exp(scores - row_max[..., None])
        denominator = jnp.sum(weights, axis=2)
        weighted = jnp.einsum(
            "rgt,td->rgd",
            weights.astype(jnp.bfloat16),
            value_one,
            preferred_element_type=jnp.float32,
        )
        return (
            (weighted / denominator[..., None]).astype(jnp.bfloat16),
            row_max + jnp.log(denominator),
        )

    outs, log_total = lax.map(one_head, (query_heads, key_heads, value_heads))
    outs = jnp.transpose(outs, (1, 0, 2, 3)).reshape(row_count, kv_count * group_size * HD)
    log_total = jnp.transpose(log_total, (1, 0, 2)).reshape(row_count, kv_count * group_size)
    return (outs, log_total)


def suffix_partial(query_rows, suffix_kv, suffix_len):
    row_count = suffix_kv.shape[0]
    length = suffix_kv.shape[2]
    kv_count = suffix_kv.shape[3] // HD
    group_size = query_rows.shape[1] // suffix_kv.shape[3]
    query_heads = query_rows.reshape(row_count, kv_count, group_size, HD)
    key_heads = suffix_kv[:, 0].reshape(row_count, length, kv_count, HD)
    value_heads = suffix_kv[:, 1].reshape(row_count, length, kv_count, HD)
    scores = (
        jnp.einsum("skgd,stkd->skgt", query_heads, key_heads, preferred_element_type=jnp.float32)
        * score_scale
    )
    is_live = (jnp.arange(length, dtype=jnp.int32)[None, :] < suffix_len[:, None])[:, None, None, :]
    row_max = jnp.max(jnp.where(is_live, scores, -jnp.inf), axis=3)
    weights = jnp.where(is_live, jnp.exp(scores - row_max[..., None]), 0.0)
    denominator = jnp.sum(weights, axis=3)
    weighted = jnp.einsum(
        "skgt,stkd->skgd",
        weights.astype(jnp.bfloat16),
        value_heads,
        preferred_element_type=jnp.float32,
    )
    outs = (weighted / denominator[..., None]).reshape(row_count, kv_count * group_size, HD)
    return (outs, (row_max + jnp.log(denominator)).reshape(row_count, kv_count * group_size))


def combine_parts(prefix_out, prefix_log, suffix_out, suffix_log):
    row_count = prefix_out.shape[0]
    heads = prefix_log.shape[1]
    joint_max = jnp.maximum(prefix_log, suffix_log)
    prefix_share = jnp.exp(prefix_log - joint_max)
    suffix_share = jnp.exp(suffix_log - joint_max)
    merged = (
        prefix_share[..., None] * prefix_out.reshape(row_count, heads, HD).astype(jnp.float32)
        + suffix_share[..., None] * suffix_out
    ) / (prefix_share + suffix_share)[..., None]
    return merged.reshape(row_count, heads * HD).astype(jnp.bfloat16)


def pick_rows(carry, piece, wanted):
    inside = (wanted >= 0) & (wanted < piece.shape[0])
    taken = jnp.take(piece, jnp.clip(wanted, 0, piece.shape[0] - 1), axis=0)
    return jnp.where(inside[:, None], taken, carry)


def shards(
    queries,
    prefix_kv,
    suffix_kv,
    suffix_len,
    prefill_group,
    sampler_groups,
    out_weight,
    norm_gain,
    residual,
):
    samples = queries.shape[0]
    own_group = lax.axis_index("grp")
    owners = sample_owners(prefill_group, sampler_groups, samples)
    groups = owners.shape[0]
    prompt_ids = jnp.arange(groups, dtype=jnp.int32)
    slot_count = sampler_groups.shape[1]
    slot_ids = jnp.arange(slot_count, dtype=jnp.int32)
    own_owners = lax.dynamic_index_in_dim(owners, own_group, 0, keepdims=False)
    own_prompt = jnp.sum(jnp.where(prefill_group == own_group, prompt_ids, 0))
    own_samplers = lax.dynamic_index_in_dim(sampler_groups, own_prompt, 0, keepdims=False)
    prefix_keys = prefix_kv[0, 0]
    prefix_values = prefix_kv[0, 1]
    row_ids = jnp.arange(samples, dtype=jnp.int32)
    wanted_rows = (own_samplers[:, None] * samples + row_ids[None, :]).reshape(-1)
    empty_rows = jnp.zeros((slot_count * samples, queries.shape[1]), queries.dtype)
    compact = pick_rows(empty_rows, lax.all_gather(queries, "grp", axis=0, tiled=True), wanted_rows)
    outs, log_total = prefix_partial(compact, prefix_keys, prefix_values)
    row_prompt = jnp.sum(
        jnp.where(prefill_group[None, :] == own_owners[:, None], prompt_ids[None, :], 0), axis=1
    )
    row_samplers = jnp.take(sampler_groups, row_prompt, axis=0)
    row_slot = jnp.sum(jnp.where(row_samplers == own_group, slot_ids[None, :], 0), axis=1)
    wanted_results = own_owners * (slot_count * samples) + row_slot * samples + row_ids
    empty_out = (
        jnp.zeros((samples, outs.shape[1]), jnp.float32),
        jnp.zeros((samples, log_total.shape[1]), jnp.float32),
    )
    prefix_out = pick_rows(
        empty_out[0],
        lax.all_gather(
            outs.astype(jnp.float32).astype(jnp.bfloat16), "grp", axis=0, tiled=True
        ).astype(jnp.float32),
        wanted_results,
    )
    prefix_log = pick_rows(
        empty_out[1],
        lax.all_gather(log_total.astype(jnp.bfloat16), "grp", axis=0, tiled=True).astype(
            jnp.float32
        ),
        wanted_results,
    )
    suffix_out, suffix_log = suffix_partial(queries, suffix_kv, suffix_len)
    attended = combine_parts(prefix_out, prefix_log, suffix_out, suffix_log)
    partial_proj = jnp.dot(attended, out_weight, preferred_element_type=jnp.float32)
    projected = lax.psum_scatter(
        partial_proj.astype(jnp.bfloat16), "tp", scatter_dimension=1, tiled=True
    ).astype(jnp.float32)
    squares = lax.psum(jnp.sum(projected * projected, axis=1), "tp")
    scale = lax.rsqrt(squares[:, None] / D + norm_eps)
    return (residual.astype(jnp.float32) + projected * scale * norm_gain[None, :]).astype(
        jnp.bfloat16
    )


def solution(mesh):
    in_specs = (
        P("grp", "tp"),
        P("grp", None, None, "tp"),
        P("grp", None, None, "tp"),
        P("grp"),
        P(),
        P(),
        P("tp", None),
        P("tp"),
        P("grp", "tp"),
    )
    out_specs = P("grp", "tp")
    return jax.shard_map(shards, mesh=mesh, in_specs=in_specs, out_specs=out_specs, check_vma=False)
```

profile of v0, /device:TPU:1, one launch (start us, length us, event | category | flops | bytes accessed | tf_op | source)
XLA Modules:
  0.0 382.1 jit_solution(12738615556688682121)
XLA Ops:
  6.5 0.7 all-gather.4.cloned.1.call-update
  7.3 0.7 fusion.19
  8.0 0.2 reduce_window_sum.11
  8.3 0.1 convert_subtract_fusion
  8.4 1.3 compare_select_fusion.6
  11.6 0.9 multiply_reduce_fusion
  12.5 0.1 fusion.37
  12.6 0.1 min.34
  12.7 0.1 min.32
  12.7 0.1 fusion.40
  12.8 0.1 and.65
  12.9 1.7 fusion.56
  14.6 0.5 copy.80
  15.2 0.5 copy.81
  15.8 113.2 %all-gather.4.cloned.1.call-done = bf16[1024,1024]{1,0:T(8,128)(2,1)} async-done(((bf16[16,1024]{1,0:T(8,128)(2,1)}), bf16[1024,1024]{1,0:T(8,128)(2,1)}) %all-gather.4.cloned.1.call-update) | async-done | bytes 2097168 | tf_op jit(solution)/shard_map/all_gather | solution.py:138
  128.9 2.7 gather_fusion.1
  131.7 0.1 fusion.18
  131.8 5.9 %while.12 = (s32[]{:T(128)}, bf16[4,64,2,128]{3,1,2,0:T(8,128)(2,1)}, bf16[4,64,2]{1,2,0:T(2,128)(2,1)S(1)}, bf16[4,64,2,128]{3,1,2,0:T(8,128)(2,1)S(1)}, bf16[4...) while((s32[]{:T(128)}, bf16[4,64,2,128]{3,1,2,0:T(8,128)(2,1)}, ...), condition=%wide.region_10.11_spmd, body=%wide.region_7.10_spmd.sunk | while | flops 67927936 | bytes 2171473 | solution.py:61
  131.8 0.3 fusion.67
  132.1 0.2 fusion.68
  132.3 0.9 fusion.69
  133.2 0.3 fusion.67
  133.5 0.2 fusion.68
  133.8 0.9 fusion.69
  134.7 0.3 fusion.67
  135.0 0.2 fusion.68
  135.3 0.9 fusion.69
  136.2 0.3 fusion.67
  136.5 0.2 fusion.68
  136.7 0.9 fusion.69
  137.6 1.0 copy.73
  138.7 0.7 reshape.428
  139.5 0.1 copy.61
  139.6 0.1 fusion.57
  139.7 0.1 reshape_squeeze.14
  139.8 0.1 iota_compare_fusion.1
  139.9 0.5 select_reduce_fusion.1
  140.4 0.1 copy.70
  140.5 0.3 fusion.41
  140.8 0.1 copy.69
  140.9 0.1 copy.72
  141.0 0.1 reshape_squeeze.15
  141.1 0.3 convolution_divide_fusion.1
  141.5 0.4 add_select_fusion
  142.0 1.3 select_reduce_fusion
  143.3 0.2 select_reduce_fusion.3
  143.5 0.6 gather_fusion
  144.1 0.2 select_reduce_fusion.2
  144.3 151.6 %all-gather = bf16[64,64,8]{1,2,0:T(8,128)(2,1)S(1)} all-gather(bf16[1,64,8]{1,2,0:T(8,128)(2,1)S(1)} %bitcast.115), channel_id=1, replica_groups=mesh['grp'=64,'tp'=4] {'grp'}, dimensions={0}, use_global_device_ids=true | all-gather | bytes 66560 | tf_op jit(solution)/shard_map/all_gather | solution.py:159
  296.0 0.4 copy.67
  296.3 0.6 gather_fusion.2
  296.9 0.1 fusion.52
  297.0 11.3 %convert_element_type.62 = f32[4096,1024]{1,0:T(8,128)} convert(bf16[4096,1024]{1,0:T(8,128)(2,1)} %all-gather.6.cloned.1.call-done) | non-fusion elementwise | flops 4194304 | bytes 25165824 | tf_op jit(solution)/shard_map/convert_element_type | solution.py:154
  308.3 6.4 %gather_fusion.3 = f32[16,1024]{1,0:T(8,128)S(1)} fusion(f32[4096,1024]{1,0:T(8,128)} %convert_element_type.62, s32[1024]{0:T(1024)S(1)} %pad_clamp_fusion), kind=kCustom, calls=%fused_computation.3 | custom fusion | bytes 131136 | tf_op jit(solution)/shard_map/jit(_take)/gather | solution.py:108
  314.6 0.1 mul.118
  314.7 0.1 mul.121
  314.8 0.1 div.32
  314.9 5.1 %convolution_convert_fusion = bf16[16,4608]{1,0:T(8,128)(2,1)S(1)} fusion(bf16[1024,4608]{1,0:T(8,128)(2,1)} %param.17, f32[2,8,8,128]{3,2,1,0:T(8,128)S(1)} %bitcast.108, f32[16,1024]{1,0:T(8,128)S(1)} %reshape.429, f32[2,8,8,128]{3,2,1,0:T(8,128)S(1)} %bitcast.107, f32[2,8,8,128]{3,2,1,0:T(8,128)S(1)} %bitcast.106, f32[16,1024]{1,0:T(8,128)S(1)} %gather_fusion.3, ...), kind=kOutput, calls=%fused_computation.22 | convolution fusion | flops 151183360 | bytes 9912352 | tf_op jit(solution)/shard_map/dot_general | solution.py:166
  320.0 1.4 copy.76
  321.4 46.9 %reduce-scatter.4.cloned.1.call-done = bf16[1152,16]{1,0:T(8,128)(2,1)} async-done(((bf16[4608,16]{1,0:T(8,128)(2,1)}), bf16[1152,16]{1,0:T(8,128)(2,1)}) %reduce-scatter.4.cloned.1.call-update) | async-done | bytes 36880
  368.3 1.1 copy.77
  369.4 0.1 fusion.20
  369.5 5.4 %psum.7 = f32[16]{0:T(128)S(1)} all-reduce(f32[16]{0:T(128)S(1)} %fusion.20), channel_id=1, replica_groups=mesh['grp'=64,'tp'=4] {'tp'}, use_global_device_ids=true, to_apply=%region_15.16 | all-reduce | flops 16 | bytes 128 | tf_op jit(solution)/shard_map/psum | solution.py:170
  374.9 0.7 fusion.23
  (44 shorter events, 0.5 us)
Async XLA Ops:
  6.5 122.4 %all-gather.4.cloned.1.call-start = ((), (), s32[]{:S(2)}) async-start(), calls=%async_computation.1 | async-start | bytes 2129920 | tf_op jit(solution)/shard_map/all_gather | solution.py:138
  7.3 289.7 %all-gather.6.cloned.1.call-start = ((), (), s32[]{:S(2)}) async-start(), calls=%async_computation.2 | async-start | bytes 8519680 | tf_op jit(solution)/shard_map/all_gather | solution.py:152
  14.6 124.9 %copy-start.3 = (s32[64,4]{0,1:T(4,128)S(1)}, s32[64,4]{0,1:T(4,128)}, u32[]{:S(2)}) copy-start(s32[64,4]{0,1:T(4,128)} %param.16) | copy-start | bytes 3076
  14.6 125.0 %copy-start.1 = (bf16[16,1024]{1,0:T(8,128)(2,1)S(1)}, bf16[16,1024]{1,0:T(8,128)(2,1)}, u32[]{:S(2)}) copy-start(bf16[16,1024]{1,0:T(8,128)(2,1)} %param.11) | copy-start | bytes 98308
  15.7 123.9 %copy-start = (bf16[16,2,32,512]{3,2,1,0:T(8,128)(2,1)S(1)}, bf16[16,2,32,512]{3,2,1,0:T(8,128)(2,1)}, u32[]{:S(2)}) copy-start(bf16[16,2,32,512]{3,2,1,0:T(8,128)(2,1)} %param.13) | copy-start | bytes 3145732
  15.7 124.1 %copy-start.6 = (s32[16]{0:T(128)S(1)}, s32[16]{0:T(128)}, u32[]{:S(2)}) copy-start(s32[16]{0:T(128)} %param.14) | copy-start | bytes 196
  131.8 10.2 %copy-start.5 = (s32[64]{0:T(128)S(1)}, s32[64]{0:T(128)}, u32[]{:S(2)}) copy-start(s32[64]{0:T(128)} %param.15) | copy-start | bytes 772
  139.4 228.9 %reduce-scatter.4.cloned.1.call-start = ((), (), s32[]{:S(2)}) async-start(), calls=%async_computation.3 | async-start | bytes 1474560
  314.9 60.0 %copy-start.2 = (bf16[16,1152]{1,0:T(8,128)(2,1)S(1)}, bf16[16,1152]{1,0:T(8,128)(2,1)}, u32[]{:S(2)}) copy-start(bf16[16,1152]{1,0:T(8,128)(2,1)} %param.19) | copy-start | bytes 110596
  314.9 60.0 %copy-start.4 = (f32[1152]{0:T(1024)S(1)}, f32[1152]{0:T(1024)}, u32[]{:S(2)}) copy-start(f32[1152]{0:T(1024)} %param.18) | copy-start | bytes 13828
Sparse Core Ops, SparseCore 0:
  10.9 117.9 all-gather.3
  139.5 145.5 all-gather.5
  321.5 46.6 reduce-scatter.3
where the time goes:
time: 383 us; the launch traced here: 382 us
  waiting for transfers between devices  161 us (42%)
  blocking collectives  157 us (41%)
  other arithmetic  19.2 us (5%)
  local copies, waits for them, and re-layouts  19 us (5%)
  between operations  15.3 us (4%)
  matrix products  10.7 us (3%)
    all_gather x1, blocking collectives, shards(): lax.all_gather(log_total.astype(jnp.bfloat16), 'grp', axis=0, tiled=True)  152 us
    all_gather x1, waiting for transfers between devices, shards(): lax.all_gather(queries, 'grp', axis=0, tiled=True)  113 us
    unnamed x4, waiting for transfers between devices  47.6 us
    convert_element_type x1, other arithmetic, shards(): prefix_out = pick_rows(empty_out[0], lax.all_gather(outs.astype(jnp.float...  11.3 us
    gather x4, local copies, waits for them, and re-layouts, pick_rows(): taken = jnp.take(piece, jnp.clip(wanted, 0, piece.shape[0] - 1), axis=0)  9.67 us
  transfers between devices with their start and end apart: 3, of which 2 were waited for; matrix products, arithmetic and copies ran while one was open for 3% of the time, Pallas kernels for 0%

commit v1 on v0

v1 whole, which is shorter than its diff:
```python
import jax
import jax.numpy as jnp
from jax import lax
from jax.experimental import pallas as pl
from jax.experimental.pallas import tpu as pltpu
from jax.sharding import PartitionSpec as P

MESH = pl.DeviceIdType.MESH
D = 4608
HD = 128
SAMP = 16
SLOTS = 4
PREFIX = 1024
SUF = 32
HEADS = 8
KVHEADS = 4
COLS = 1152
PROMPTS = 64
SCORE_SCALE = 144.0 ** (-0.5)
NORM_EPS = 1e-06
NEG = -1e30

Z_FAR = (4, 3, 5, 2, 6, 1, 7)
Z_NEAR = (1, 7, 2, 6, 3, 5, 4)
B_FAR = ((2, 1), (1, 1), (3, 1), (2, 0), (0, 1), (1, 0), (3, 0))

f32 = jnp.float32
bf16 = jnp.bfloat16
i32 = jnp.int32


def kernel(
    q_hbm, kv_hbm, suf_hbm, len_hbm, pre_hbm, sam_hbm, w_hbm, gain_hbm, res_hbm,
    o_ref,
    qh, kv, suf, w, gain, res, len_s, pre_s, sam_s, sam_v,
    own_p, pick_s,
    qall, csend, qc, rsend, rc, bsend, bt, asend, fin,
    hot, hot2, lmask, suf_o, suf_l, psend, pr, sqs, sqr,
    lq, lkv, lsuf, lw, lsmall, lint,
    sa, ra, sb, rb, sc, rcs, sct, rct, sbt, rbt, sat, rat, srs, rrs, ssq, rsq,
):
    me = lax.axis_index("grp")
    tp = lax.axis_index("tp")
    x = me // 16
    z = (me // 2) % 8
    yh = me % 2
    b = x * 2 + yh

    def grp_of(xx, zz, yy):
        return (xx * 8 + zz) * 2 + yy

    def z_peer(off):
        zz = (z + off) % 8
        return zz, (grp_of(x, zz, yh), tp)

    def b_peer(off):
        xx = (x + off[0]) % 4
        yy = (yh + off[1]) % 2
        return xx * 2 + yy, (grp_of(xx, z, yy), tp)

    def tp_peer(off):
        yy, cc = (tp // 2 + off // 2) % 2, (tp % 2 + off % 2) % 2
        return yy * 2 + cc, (me, yy * 2 + cc)

    def remote(src, dst, send, recv, device):
        return pltpu.make_async_remote_copy(
            src_ref=src, dst_ref=dst, send_sem=send, recv_sem=recv,
            device_id=device, device_id_type=MESH,
        )

    barrier = pltpu.get_barrier_semaphore()
    for off in Z_FAR:
        pl.semaphore_signal(barrier, inc=1, device_id=z_peer(off)[1], device_id_type=MESH)
    for off in B_FAR:
        pl.semaphore_signal(barrier, inc=1, device_id=b_peer(off)[1], device_id_type=MESH)
    for off in (2, 3, 1):
        pl.semaphore_signal(barrier, inc=1, device_id=tp_peer(off)[1], device_id_type=MESH)

    ints = [
        pltpu.make_async_copy(pre_hbm, pre_s, lint.at[0]),
        pltpu.make_async_copy(sam_hbm, sam_s, lint.at[1]),
        pltpu.make_async_copy(sam_hbm, sam_v, lint.at[2]),
        pltpu.make_async_copy(len_hbm, len_s, lint.at[3]),
    ]
    for copy in ints:
        copy.start()
    for i in range(HEADS):
        pltpu.make_async_copy(q_hbm.at[:, pl.ds(i * HD, HD)], qh.at[i], lq).start()
    for part in range(2):
        for k in range(KVHEADS):
            pltpu.make_async_copy(
                kv_hbm.at[0, part, :, pl.ds(k * HD, HD)], kv.at[part, k], lkv
            ).start()
    for part in range(2):
        for k in range(KVHEADS):
            pltpu.make_async_copy(
                suf_hbm.at[:, part, :, pl.ds(k * HD, HD)], suf.at[part, k], lsuf
            ).start()
    small = [
        pltpu.make_async_copy(gain_hbm, gain, lsmall.at[0]),
        pltpu.make_async_copy(res_hbm, res, lsmall.at[1]),
    ]
    for copy in small:
        copy.start()
    for t in range(4):
        pltpu.make_async_copy(w_hbm.at[:, pl.ds(t * COLS, COLS)], w.at[t], lw).start()

    for copy in ints:
        copy.wait()

    line = [z_peer(off)[1][0] for off in range(8)]

    def find(p, found):
        group = pre_s[p]
        return tuple(found[off] + jnp.where(group == line[off], p, 0) for off in range(8))

    found = lax.fori_loop(0, PROMPTS, find, (jnp.int32(0),) * 8)
    for off in range(8):
        own_p[off] = found[off]
        for s in range(SLOTS):
            pick_s[off * SLOTS + s] = sam_s[s, found[off] & 63]

    pltpu.make_async_copy(qh, qh, lq).wait()
    pl.semaphore_wait(barrier, 17)

    for off in Z_FAR:
        zz, device = z_peer(off)
        remote(qh.at[zz], qall.at[off], sa, ra.at[off], device).start()
    qall[0] = qh[z]

    for off in (0,) + Z_NEAR:
        block = qall.at[off]
        if off != 0:
            remote(qh.at[0], block, sa, ra.at[off], (me, tp)).wait_recv()
        for boff in B_FAR:
            slot = (boff[0] * 2 + boff[1]) * 8 + off
            remote(block, qall.at[slot], sb, rb, b_peer(boff)[1]).start()
    others = qall.at[pl.ds(8, 56)]
    remote(others, others, sb, rb, (me, tp)).wait_recv()

    for off in Z_FAR + (0,):
        for s in range(SLOTS):
            g = pick_s[off * SLOTS + s]
            slot = (((x - (g >> 4)) & 3) * 2 + ((yh - g) & 1)) * 8 + ((z - (g >> 1)) & 7)
            block = qall[slot]
            if off == 0:
                qc[0, pl.ds(s * SAMP, SAMP)] = block
            else:
                csend[off, pl.ds(s * SAMP, SAMP)] = block
        if off != 0:
            remote(csend.at[off], qc.at[off], sc, rcs.at[off], z_peer(off)[1]).start()

    lane = lax.broadcasted_iota(i32, (1, 512), 1)
    lane_block = lane >> 4
    lane_row = lane & 15
    group_lane = jnp.zeros((1, 512), i32)
    prompt_lane = jnp.zeros((1, 512), i32)
    for c in range(32):
        group_lane = jnp.where(lane_block == c, pick_s[c], group_lane)
    for off in range(8):
        prompt_lane = jnp.where((lane >> 6) == off, own_p[off], prompt_lane)
    pick_b = (((group_lane >> 4) - x) & 3) * 2 + ((group_lane - yh) & 1)
    pick_z = ((group_lane >> 1) - z) & 7
    table = jnp.transpose(sam_v[...])
    member = jnp.zeros((PROMPTS, 512), f32)
    for s in range(SLOTS):
        member = member + jnp.where(table[:, s : s + 1] == group_lane, 1.0, 0.0)
    prompt_row = lax.broadcasted_iota(i32, (PROMPTS, 512), 0)
    count = jnp.sum(member, axis=0, keepdims=True)
    rank = jnp.sum(jnp.where(prompt_row < prompt_lane, member, 0.0), axis=0, keepdims=True)
    row = lane_row.astype(f32)
    rest = row - jnp.floor((row + 0.5) / count) * count
    owned = rest == rank
    place = jnp.where(owned, (pick_b * 8 + pick_z) * SAMP + lane_row, -1)
    place2 = jnp.where(owned, pick_b * SAMP + lane_row, -1)
    rows = lax.broadcasted_iota(i32, (128, 512), 0)
    for bb in range(8):
        hot[bb] = jnp.where(rows + bb * 128 == place, 1.0, 0.0).astype(bf16)
    hot2[...] = jnp.where(rows == place2, 1.0, 0.0).astype(bf16)
    tile_lane = lax.broadcasted_iota(i32, (SAMP, HD), 1)
    for c in range(32):
        of_z = ((pick_s[c] >> 1) - z) & 7
        keep = ((tile_lane >> 3) == of_z) & (((tile_lane & 7) >> 1) == c % SLOTS)
        lmask[pl.ds(c * SAMP, SAMP)] = jnp.where(keep, 1.0, 0.0).astype(bf16)

    pltpu.make_async_copy(kv, kv, lkv).wait()
    for off in (0,) + Z_NEAR:
        if off != 0:
            remote(csend.at[off], qc.at[off], sc, rcs.at[off], (me, tp)).wait_recv()
        head, device = z_peer(-off)
        k = head // 2
        scores = (
            lax.dot_general(
                qc[off], kv[0, k], (((1,), (1,)), ((), ())), preferred_element_type=f32
            )
            * SCORE_SCALE
        )
        top = jnp.max(scores, axis=1, keepdims=True)
        weights = jnp.exp(scores - top)
        total = jnp.sum(weights, axis=1, keepdims=True)
        out = jnp.dot(weights.astype(bf16), kv[1, k], preferred_element_type=f32) / total
        log_total = top + jnp.log(total)
        high = log_total.astype(bf16).astype(f32)
        low = log_total - high
        tile = jnp.zeros((SAMP, HD), f32)
        for s in range(SLOTS):
            at = s * SAMP
            tile = jnp.where((tile_lane & 7) == 2 * s, high[at : at + SAMP], tile)
            tile = jnp.where((tile_lane & 7) == 2 * s + 1, low[at : at + SAMP], tile)
        result = rc if off == 0 else rsend
        result[off, pl.ds(0, 64)] = out.astype(bf16)
        result[off, pl.ds(64, SAMP)] = tile.astype(bf16)
        if off != 0:
            remote(rsend.at[off], rc.at[off], sct, rct, device).start()

    pltpu.make_async_copy(suf, suf, lsuf).wait()
    col = lax.broadcasted_iota(i32, (32, 512), 1)
    srow = lax.broadcasted_iota(i32, (32, 512), 0) & 15
    col_sample = col >> 5
    live_len = jnp.zeros((32, 512), i32)
    for s in range(SAMP):
        live_len = jnp.where(col_sample == s, len_s[s], live_len)
    live = (col_sample == srow) & ((col & 31) < live_len)
    for k in range(KVHEADS):
        query = qh[pl.ds(2 * k, 2)].reshape(32, HD)
        scores = (
            lax.dot_general(
                query, suf[0, k].reshape(512, HD), (((1,), (1,)), ((), ())),
                preferred_element_type=f32,
            )
            * SCORE_SCALE
        )
        top = jnp.max(jnp.where(live, scores, NEG), axis=1, keepdims=True)
        weights = jnp.where(live, jnp.exp(jnp.where(live, scores - top, 0.0)), 0.0)
        total = jnp.sum(weights, axis=1, keepdims=True)
        out = (
            jnp.dot(weights.astype(bf16), suf[1, k].reshape(512, HD), preferred_element_type=f32)
            / total
        )
        suf_o[pl.ds(k * 32, 32)] = out
        suf_l[pl.ds(k * 32, 32)] = jnp.broadcast_to(top + jnp.log(total), (32, HD))

    seven = rc.at[pl.ds(1, 7)]
    remote(seven, seven, sct, rct, (me, tp)).wait_recv()
    results = rc[:, pl.ds(0, 64)].reshape(512, HD)
    logs = jnp.concatenate(
        [rc[off, pl.ds(64, SAMP)] for off in range(8) for _ in range(SLOTS)], axis=0
    ) * lmask[...]
    log_rows = jnp.dot(hot2[...], logs, preferred_element_type=f32).astype(bf16)

    for boff in B_FAR + ((0, 0),):
        n = boff[0] * 2 + boff[1]
        picked = jnp.dot(hot[n], results, preferred_element_type=f32).astype(bf16)
        block = bt if n == 0 else bsend
        block[n, pl.ds(0, 128)] = picked
        block[n, pl.ds(128, SAMP)] = log_rows[n * SAMP : (n + 1) * SAMP]
        if n != 0:
            remote(bsend.at[n], bt.at[n], sbt, rbt, b_peer(boff)[1]).start()
    seven = bt.at[pl.ds(1, 7)]
    remote(seven, seven, sbt, rbt, (me, tp)).wait_recv()

    merged = bt[0].astype(f32)
    for n in range(1, 8):
        merged = merged + bt[n].astype(f32)
    merged = merged.astype(bf16)
    for off in Z_FAR + (0,):
        block = fin if off == 0 else asend
        block[off, pl.ds(0, SAMP)] = merged[off * SAMP : (off + 1) * SAMP]
        block[off, pl.ds(SAMP, SAMP)] = merged[128:144]
        if off != 0:
            remote(asend.at[off], fin.at[off], sat, rat, z_peer(off)[1]).start()
    pltpu.make_async_copy(w, w, lw).wait()
    seven = fin.at[pl.ds(1, 7)]
    remote(seven, seven, sat, rat, (me, tp)).wait_recv()

    come = [fin[(z - i) % 8] for i in range(HEADS)]
    prefix_out = jnp.concatenate([block[:SAMP] for block in come], axis=0).astype(f32)
    log_tile = jnp.concatenate([block[SAMP:] for block in come], axis=0).astype(f32)
    all_lane = lax.broadcasted_iota(i32, (128, HD), 1)
    all_row = lax.broadcasted_iota(i32, (128, HD), 0)
    prefix_log = jnp.sum(
        jnp.where((all_lane >> 3) == ((z - (all_row >> 4)) & 7), log_tile, 0.0),
        axis=1, keepdims=True,
    )
    suffix_log = suf_l[...]
    joint = jnp.maximum(prefix_log, suffix_log)
    share_p = jnp.exp(prefix_log - joint)
    share_s = jnp.exp(suffix_log - joint)
    attended = (
        (share_p * prefix_out + share_s * suf_o[...]) / (share_p + share_s)
    ).astype(bf16)
    attended = jnp.concatenate(
        [attended[i * SAMP : (i + 1) * SAMP] for i in range(HEADS)], axis=1
    )

    for off in (2, 3, 1):
        tt, device = tp_peer(off)
        psend[off - 1] = jnp.dot(attended, w[tt], preferred_element_type=f32).astype(bf16)
        remote(psend.at[off - 1], pr.at[off - 1], srs, rrs, device).start()
    projected = jnp.dot(attended, w[tp], preferred_element_type=f32)
    remote(psend, pr, srs, rrs, (me, tp)).wait_recv()
    for off in range(3):
        projected = projected + pr[off].astype(f32)
    squares = jnp.zeros((SAMP, HD), f32)
    for n in range(COLS // HD):
        piece = projected[:, n * HD : (n + 1) * HD]
        squares = squares + piece * piece
    sqs[...] = squares
    for off in (2, 3, 1):
        remote(sqs, sqr.at[off - 1], ssq.at[off - 1], rsq, tp_peer(off)[1]).start()
    for copy in small:
        copy.wait()
    remote(sqr, sqr, ssq.at[0], rsq, (me, tp)).wait_recv()
    for off in range(3):
        squares = squares + sqr[off]
    scale = lax.rsqrt(jnp.sum(squares, axis=1, keepdims=True) / D + NORM_EPS)
    o_ref[...] = (res[...].astype(f32) + projected * scale * gain[...].reshape(1, COLS)).astype(bf16)

    seven = qall.at[pl.ds(0, 7)]
    remote(seven, seven, sa, ra.at[0], (me, tp)).wait_send()
    seven = qall.at[pl.ds(0, 56)]
    remote(seven, seven, sb, rb, (me, tp)).wait_send()
    for ref, send, recv in (
        (csend, sc, rcs.at[0]), (rc, sct, rct), (bt, sbt, rbt), (fin, sat, rat)
    ):
        seven = ref.at[pl.ds(0, 7)]
        remote(seven, seven, send, recv, (me, tp)).wait_send()
    remote(psend, pr, srs, rrs, (me, tp)).wait_send()
    for off in range(3):
        remote(sqs, sqr.at[off], ssq.at[off], rsq, (me, tp)).wait_send()


def shards(
    queries, prefix_kv, suffix_kv, suffix_len, prefill_group, sampler_groups,
    out_weight, norm_gain, residual,
):
    vmem = pltpu.VMEM
    dma = pltpu.SemaphoreType.DMA
    scratch = [
        vmem((HEADS, SAMP, HD), bf16),
        vmem((2, KVHEADS, PREFIX, HD), bf16),
        vmem((2, KVHEADS, SAMP, SUF, HD), bf16),
        vmem((4, HEADS * HD, COLS), bf16),
        vmem((COLS,), f32),
        vmem((SAMP, COLS), bf16),
        pltpu.SMEM((SAMP,), i32),
        pltpu.SMEM((PROMPTS,), i32),
        pltpu.SMEM((SLOTS, PROMPTS), i32),
        vmem((SLOTS, PROMPTS), i32),
        pltpu.SMEM((8,), i32),
        pltpu.SMEM((32,), i32),
        vmem((64, SAMP, HD), bf16),
        vmem((8, 64, HD), bf16),
        vmem((8, 64, HD), bf16),
        vmem((8, 80, HD), bf16),
        vmem((8, 80, HD), bf16),
        vmem((8, 144, HD), bf16),
        vmem((8, 144, HD), bf16),
        vmem((8, 32, HD), bf16),
        vmem((8, 32, HD), bf16),
        vmem((8, 128, 512), bf16),
        vmem((128, 512), bf16),
        vmem((512, HD), bf16),
        vmem((128, HD), f32),
        vmem((128, HD), f32),
        vmem((3, SAMP, COLS), bf16),
        vmem((3, SAMP, COLS), bf16),
        vmem((SAMP, HD), f32),
        vmem((3, SAMP, HD), f32),
        dma, dma, dma, dma, dma((2,)), dma((4,)),
        dma, dma((8,)),
        dma, dma,
        dma, dma((8,)),
        dma, dma,
        dma, dma,
        dma, dma,
        dma, dma,
        dma((3,)), dma,
    ]
    anywhere = pl.BlockSpec(memory_space=pl.ANY)
    return pl.pallas_call(
        kernel,
        out_shape=jax.ShapeDtypeStruct(residual.shape, bf16),
        in_specs=[anywhere] * 9,
        out_specs=pl.BlockSpec(memory_space=pltpu.VMEM),
        scratch_shapes=scratch,
        compiler_params=pltpu.CompilerParams(
            collective_id=0, has_side_effects=True, vmem_limit_bytes=63 * 1024 * 1024
        ),
        cost_estimate=pl.CostEstimate(
            flops=500_000_000, bytes_accessed=13_000_000, transcendentals=600_000
        ),
    )(
        queries, prefix_kv, suffix_kv, suffix_len, prefill_group, sampler_groups.T,
        out_weight, norm_gain, residual,
    )


def solution(mesh):
    in_specs = (
        P("grp", "tp"),
        P("grp", None, None, "tp"),
        P("grp", None, None, "tp"),
        P("grp"),
        P(),
        P(),
        P("tp", None),
        P("tp"),
        P("grp", "tp"),
    )
    return jax.shard_map(
        shards, mesh=mesh, in_specs=in_specs, out_specs=P("grp", "tp"), check_vma=False
    )
```

time: 383 us -> 51.1 us (0.13)
  waiting for transfers between devices: 161 us -> 0 us
  blocking collectives: 157 us -> 0 us
  Pallas kernels: 0 us -> 49.5 us
  other arithmetic: 19.2 us -> 0 us
  local copies, waits for them, and re-layouts: 19 us -> 1.39 us
  between operations: 15.3 us -> 0.01 us
  matrix products: 10.7 us -> 0 us
    all_gather x1 -> x0, blocking collectives: 152 us -> none  [shards(): lax.all_gather(log_total.astype(jnp.bfloat16), 'grp', axis=0, tiled=True)]
    all_gather x2 -> x0, waiting for transfers between devices: 113 us -> none  [the longest x1 113 us: shards(): lax.all_gather(queries, 'grp', axis=0, tiled=True)]
    pallas_call x0 -> x1, Pallas kernels: none -> 49.5 us  [shards(): pl.pallas_call(kernel, out_shape=jax.ShapeDtypeStruct(residual.shape, bf1...]
    unnamed x4 -> x0, waiting for transfers between devices: 47.6 us -> none
    convert_element_type x2 -> x0, other arithmetic: 12 us -> none  [the longest x1 11.3 us: shards(): prefix_out = pick_rows(empty_out[0], lax.all_gather(outs.astype(jnp.float...]
    dot_general x11 -> x0, matrix products: 10.7 us -> none  [the longest x1 5.09 us: shards(): jnp.dot(attended, out_weight, preferred_element_type=jnp.float32)]
    gather x5 -> x0, local copies, waits for them, and re-layouts: 10.2 us -> none  [the longest x4 9.67 us: pick_rows(): taken = jnp.take(piece, jnp.clip(wanted, 0, piece.shape[0] - 1), axis=0)]
    psum x1 -> x0, blocking collectives: 5.4 us -> none  [shards(): squares = lax.psum(jnp.sum(projected * projected, axis=1), 'tp')]
  transfers between devices with their start and end apart: 3 -> 0, of which waited for: 2 -> 0; matrix products, arithmetic and copies ran while one was open for 3% -> 0% of each run, Pallas kernels for 0% -> 0%
where the time goes in v1:
time: 51.1 us; the launch traced here: 50.9 us
  Pallas kernels  49.5 us (97%)
  local copies, waits for them, and re-layouts  1.39 us (3%)
    pallas_call x1, Pallas kernels, shards(): pl.pallas_call(kernel, out_shape=jax.ShapeDtypeStruct(residual.shape, bf1...  49.5 us
    unnamed x1, local copies, waits for them, and re-layouts  1.39 us

profile of v1, /device:TPU:1, one launch (start us, length us, event | category | flops | bytes accessed | tf_op | source)
XLA Modules:
  0.0 50.9 jit_solution(11963971351843956380)
XLA Ops:
  0.0 49.5 %shard_map.91 = bf16[16,1152]{1,0:T(8,128)(2,1)} custom-call(bf16[16,1024]{1,0:T(8,128)(2,1)} %q_hbm.1, bf16[1,2,1024,512]{3,2,1,0:T(8,128)(2,1)} %kv_hbm.1, bf16[16,2,32,512]{3,2,1,0:T(8,128)(2,1)} %suf_hbm.1, s32[16]{0:T(128)} %len_hbm.1, s32[64]{0:T(128)} %pre_hbm.1, s32[4,64]{1,0:T(4,128)} %bitcast.1, bf16[1024,4608]{1,0:T(8,128)(2,1)} %w_hbm.1, ...), custom_call_target="tpu_custom_call" | custom-call | flops 500000000 | bytes 13000000 | tf_op jit(solution)/shard_map/pallas_call | solution.py:381
  49.5 1.4 %copy.11 = bf16[16,1152]{1,0:T(8,128)(2,1)} copy(bf16[16,1152]{1,0:T(8,128)(2,1)} %shard_map.91) | data formatting | bytes 73728

commit v2 on v1

--- a/solution.py
+++ b/solution.py
@@ -34,7 +34,7 @@
     o_ref,
     qh, kv, suf, w, gain, res, len_s, pre_s, sam_s, sam_v,
     own_p, pick_s,
-    qall, csend, qc, rsend, rc, bsend, bt, asend, fin,
+    qall, csend, qc, rsend, rc, bsend1, bsend2, bt1, bt2, asend, fin,
     hot, hot2, lmask, suf_o, suf_l, psend, pr, sqs, sqr,
     lq, lkv, lsuf, lw, lsmall, lint,
     sa, ra, sb, rb, sc, rcs, sct, rct, sbt, rbt, sat, rat, srs, rrs, ssq, rsq,
@@ -173,9 +173,12 @@
     owned = rest == rank
     place = jnp.where(owned, (pick_b * 8 + pick_z) * SAMP + lane_row, -1)
     place2 = jnp.where(owned, pick_b * SAMP + lane_row, -1)
+    few = lax.broadcasted_iota(i32, (SAMP, 512), 0)
+    for n in range(8):
+        for at, off in enumerate(Z_FAR + (0,)):
+            row_of = few + (n * 8 + off) * SAMP
+            hot[n, pl.ds(at * SAMP, SAMP)] = jnp.where(row_of == place, 1.0, 0.0).astype(bf16)
     rows = lax.broadcasted_iota(i32, (128, 512), 0)
-    for bb in range(8):
-        hot[bb] = jnp.where(rows + bb * 128 == place, 1.0, 0.0).astype(bf16)
     hot2[...] = jnp.where(rows == place2, 1.0, 0.0).astype(bf16)
     tile_lane = lax.broadcasted_iota(i32, (SAMP, HD), 1)
     for c in range(32):
@@ -184,11 +187,9 @@
         lmask[pl.ds(c * SAMP, SAMP)] = jnp.where(keep, 1.0, 0.0).astype(bf16)
 
     pltpu.make_async_copy(kv, kv, lkv).wait()
-    for off in (0,) + Z_NEAR:
-        if off != 0:
-            remote(csend.at[off], qc.at[off], sc, rcs.at[off], (me, tp)).wait_recv()
-        head, device = z_peer(-off)
-        k = head // 2
+
+    def attend(off):
+        k = z_peer(-off)[0] // 2
         scores = (
             lax.dot_general(
                 qc[off], kv[0, k], (((1,), (1,)), ((), ())), preferred_element_type=f32
@@ -207,11 +208,21 @@
             at = s * SAMP
             tile = jnp.where((tile_lane & 7) == 2 * s, high[at : at + SAMP], tile)
             tile = jnp.where((tile_lane & 7) == 2 * s + 1, low[at : at + SAMP], tile)
-        result = rc if off == 0 else rsend
-        result[off, pl.ds(0, 64)] = out.astype(bf16)
-        result[off, pl.ds(64, SAMP)] = tile.astype(bf16)
-        if off != 0:
-            remote(rsend.at[off], rc.at[off], sct, rct, device).start()
+        return out.astype(bf16), tile.astype(bf16)
+
+    for group in ((0,), (1, 7), (2, 6), (4,), (3, 5)):
+        for off in group:
+            if off != 0:
+                remote(csend.at[off], qc.at[off], sc, rcs.at[off], (me, tp)).wait_recv()
+        results = [attend(off) for off in group]
+        for off, (out, tile) in zip(group, results):
+            result = rc if off == 0 else rsend
+            result[off, pl.ds(0, 64)] = out
+            result[off, pl.ds(64, SAMP)] = tile
+            if off != 0:
+                remote(
+                    rsend.at[off], rc.at[off], sct, rct, z_peer(-off)[1]
+                ).start()
 
     pltpu.make_async_copy(suf, suf, lsuf).wait()
     col = lax.broadcasted_iota(i32, (32, 512), 1)
@@ -251,24 +262,40 @@
     for boff in B_FAR + ((0, 0),):
         n = boff[0] * 2 + boff[1]
         picked = jnp.dot(hot[n], results, preferred_element_type=f32).astype(bf16)
-        block = bt if n == 0 else bsend
-        block[n, pl.ds(0, 128)] = picked
-        block[n, pl.ds(128, SAMP)] = log_rows[n * SAMP : (n + 1) * SAMP]
+        first, second = (bt1, bt2) if n == 0 else (bsend1, bsend2)
+        first[n, pl.ds(0, 48)] = picked[:48]
+        first[n, pl.ds(48, SAMP)] = log_rows[n * SAMP : (n + 1) * SAMP]
+        second[n] = picked[48:]
         if n != 0:
-            remote(bsend.at[n], bt.at[n], sbt, rbt, b_peer(boff)[1]).start()
-    seven = bt.at[pl.ds(1, 7)]
-    remote(seven, seven, sbt, rbt, (me, tp)).wait_recv()
-
-    merged = bt[0].astype(f32)
-    for n in range(1, 8):
-        merged = merged + bt[n].astype(f32)
-    merged = merged.astype(bf16)
-    for off in Z_FAR + (0,):
-        block = fin if off == 0 else asend
-        block[off, pl.ds(0, SAMP)] = merged[off * SAMP : (off + 1) * SAMP]
-        block[off, pl.ds(SAMP, SAMP)] = merged[128:144]
+            remote(bsend1.at[n], bt1.at[n], sbt.at[0], rbt.at[0], b_peer(boff)[1]).start()
+    for boff in B_FAR:
+        n = boff[0] * 2 + boff[1]
+        remote(bsend2.at[n], bt2.at[n], sbt.at[1], rbt.at[1], b_peer(boff)[1]).start()
+
+    def merge(ref):
+        merged = ref[0].astype(f32)
+        for n in range(1, 8):
+            merged = merged + ref[n].astype(f32)
+        return merged.astype(bf16)
+
+    def give(off, block, logs):
+        ref = fin if off == 0 else asend
+        ref[off, pl.ds(0, SAMP)] = block
+        ref[off, pl.ds(SAMP, SAMP)] = logs
         if off != 0:
             remote(asend.at[off], fin.at[off], sat, rat, z_peer(off)[1]).start()
+
+    seven = bt1.at[pl.ds(1, 7)]
+    remote(seven, seven, sbt.at[0], rbt.at[0], (me, tp)).wait_recv()
+    merged = merge(bt1)
+    logs = merged[48:]
+    for at, off in enumerate(Z_FAR[:3]):
+        give(off, merged[at * SAMP : (at + 1) * SAMP], logs)
+    seven = bt2.at[pl.ds(1, 7)]
+    remote(seven, seven, sbt.at[1], rbt.at[1], (me, tp)).wait_recv()
+    merged = merge(bt2)
+    for at, off in enumerate(Z_FAR[3:] + (0,)):
+        give(off, merged[at * SAMP : (at + 1) * SAMP], logs)
     pltpu.make_async_copy(w, w, lw).wait()
     seven = fin.at[pl.ds(1, 7)]
     remote(seven, seven, sat, rat, (me, tp)).wait_recv()
@@ -321,7 +348,8 @@
     seven = qall.at[pl.ds(0, 56)]
     remote(seven, seven, sb, rb, (me, tp)).wait_send()
     for ref, send, recv in (
-        (csend, sc, rcs.at[0]), (rc, sct, rct), (bt, sbt, rbt), (fin, sat, rat)
+        (csend, sc, rcs.at[0]), (rc, sct, rct), (bt1, sbt.at[0], rbt.at[0]),
+        (bt2, sbt.at[1], rbt.at[1]), (fin, sat, rat),
     ):
         seven = ref.at[pl.ds(0, 7)]
         remote(seven, seven, send, recv, (me, tp)).wait_send()
@@ -354,8 +382,10 @@
         vmem((8, 64, HD), bf16),
         vmem((8, 80, HD), bf16),
         vmem((8, 80, HD), bf16),
-        vmem((8, 144, HD), bf16),
-        vmem((8, 144, HD), bf16),
+        vmem((8, 64, HD), bf16),
+        vmem((8, 80, HD), bf16),
+        vmem((8, 64, HD), bf16),
+        vmem((8, 80, HD), bf16),
         vmem((8, 32, HD), bf16),
         vmem((8, 32, HD), bf16),
         vmem((8, 128, 512), bf16),
@@ -372,7 +402,7 @@
         dma, dma,
         dma, dma((8,)),
         dma, dma,
-        dma, dma,
+        dma((2,)), dma((2,)),
         dma, dma,
         dma, dma,
         dma((3,)), dma,

time: 51.1 us -> 50.3 us (0.984)
  Pallas kernels: 49.5 us -> 48.8 us
    pallas_call x1, Pallas kernels: 49.5 us -> 48.8 us  [shards(): pl.pallas_call(kernel, out_shape=jax.ShapeDtypeStruct(residual.shape, bf1...]
where the time goes in v2:
time: 50.3 us; the launch traced here: 50.2 us
  Pallas kernels  48.8 us (97%)
  local copies, waits for them, and re-layouts  1.39 us (3%)
    pallas_call x1, Pallas kernels, shards(): pl.pallas_call(kernel, out_shape=jax.ShapeDtypeStruct(residual.shape, bf1...  48.8 us
    unnamed x1, local copies, waits for them, and re-layouts  1.39 us

profile of v2, /device:TPU:1, one launch (start us, length us, event | category | flops | bytes accessed | tf_op | source)
XLA Modules:
  0.0 50.2 jit_solution(8299066048278551541)
XLA Ops:
  0.0 48.8 %shard_map.91 = bf16[16,1152]{1,0:T(8,128)(2,1)} custom-call(bf16[16,1024]{1,0:T(8,128)(2,1)} %q_hbm.1, bf16[1,2,1024,512]{3,2,1,0:T(8,128)(2,1)} %kv_hbm.1, bf16[16,2,32,512]{3,2,1,0:T(8,128)(2,1)} %suf_hbm.1, s32[16]{0:T(128)} %len_hbm.1, s32[64]{0:T(128)} %pre_hbm.1, s32[4,64]{1,0:T(4,128)} %bitcast.1, bf16[1024,4608]{1,0:T(8,128)(2,1)} %w_hbm.1, ...), custom_call_target="tpu_custom_call" | custom-call | flops 500000000 | bytes 13000000 | tf_op jit(solution)/shard_map/pallas_call | solution.py:411
  48.8 1.4 %copy.11 = bf16[16,1152]{1,0:T(8,128)(2,1)} copy(bf16[16,1152]{1,0:T(8,128)(2,1)} %shard_map.91) | data formatting | bytes 73728

commit v3 on v2

--- a/solution.py
+++ b/solution.py
@@ -35,7 +35,7 @@
     qh, kv, suf, w, gain, res, len_s, pre_s, sam_s, sam_v,
     own_p, pick_s,
     qall, csend, qc, rsend, rc, bsend1, bsend2, bt1, bt2, asend, fin,
-    hot, hot2, lmask, suf_o, suf_l, psend, pr, sqs, sqr,
+    hot1, hot2, lmask, suf_o, suf_l, psend, pr, sqs, sqr,
     lq, lkv, lsuf, lw, lsmall, lint,
     sa, ra, sb, rb, sc, rcs, sct, rct, sbt, rbt, sat, rat, srs, rrs, ssq, rsq,
 ):
@@ -174,12 +174,16 @@
     place = jnp.where(owned, (pick_b * 8 + pick_z) * SAMP + lane_row, -1)
     place2 = jnp.where(owned, pick_b * SAMP + lane_row, -1)
     few = lax.broadcasted_iota(i32, (SAMP, 512), 0)
+
+    def one_hot(first, wanted):
+        return jnp.where(few + first * SAMP == wanted, 1.0, 0.0).astype(bf16)
+
     for n in range(8):
-        for at, off in enumerate(Z_FAR + (0,)):
-            row_of = few + (n * 8 + off) * SAMP
-            hot[n, pl.ds(at * SAMP, SAMP)] = jnp.where(row_of == place, 1.0, 0.0).astype(bf16)
-    rows = lax.broadcasted_iota(i32, (128, 512), 0)
-    hot2[...] = jnp.where(rows == place2, 1.0, 0.0).astype(bf16)
+        for at, off in enumerate(Z_FAR[:3]):
+            hot1[n, pl.ds(at * SAMP, SAMP)] = one_hot(n * 8 + off, place)
+        hot1[n, pl.ds(48, SAMP)] = one_hot(n, place2)
+        for at, off in enumerate(Z_FAR[3:] + (0,)):
+            hot2[n, pl.ds(at * SAMP, SAMP)] = one_hot(n * 8 + off, place)
     tile_lane = lax.broadcasted_iota(i32, (SAMP, HD), 1)
     for c in range(32):
         of_z = ((pick_s[c] >> 1) - z) & 7
@@ -210,7 +214,7 @@
             tile = jnp.where((tile_lane & 7) == 2 * s + 1, low[at : at + SAMP], tile)
         return out.astype(bf16), tile.astype(bf16)
 
-    for group in ((0,), (1, 7), (2, 6), (4,), (3, 5)):
+    for group in ((4,), (3, 5), (2, 6), (1, 7), (0,)):
         for off in group:
             if off != 0:
                 remote(csend.at[off], qc.at[off], sc, rcs.at[off], (me, tp)).wait_recv()
@@ -257,20 +261,25 @@
     logs = jnp.concatenate(
         [rc[off, pl.ds(64, SAMP)] for off in range(8) for _ in range(SLOTS)], axis=0
     ) * lmask[...]
-    log_rows = jnp.dot(hot2[...], logs, preferred_element_type=f32).astype(bf16)
+    both = jnp.concatenate([results, logs], axis=1)
+
+    def from_b(boff):
+        n = boff[0] * 2 + boff[1]
+        first, second = (bt1, bt2) if n == 0 else (bsend1, bsend2)
+        return n, first.at[n], second.at[n]
 
     for boff in B_FAR + ((0, 0),):
-        n = boff[0] * 2 + boff[1]
-        picked = jnp.dot(hot[n], results, preferred_element_type=f32).astype(bf16)
-        first, second = (bt1, bt2) if n == 0 else (bsend1, bsend2)
-        first[n, pl.ds(0, 48)] = picked[:48]
-        first[n, pl.ds(48, SAMP)] = log_rows[n * SAMP : (n + 1) * SAMP]
-        second[n] = picked[48:]
+        n, first, _ = from_b(boff)
+        picked = jnp.dot(hot1[n], both, preferred_element_type=f32).astype(bf16)
+        first[pl.ds(0, 48)] = picked[:48, :HD]
+        first[pl.ds(48, SAMP)] = picked[48:, HD:]
         if n != 0:
-            remote(bsend1.at[n], bt1.at[n], sbt.at[0], rbt.at[0], b_peer(boff)[1]).start()
-    for boff in B_FAR:
-        n = boff[0] * 2 + boff[1]
-        remote(bsend2.at[n], bt2.at[n], sbt.at[1], rbt.at[1], b_peer(boff)[1]).start()
+            remote(first, bt1.at[n], sbt.at[0], rbt.at[0], b_peer(boff)[1]).start()
+    for boff in B_FAR + ((0, 0),):
+        n, _, second = from_b(boff)
+        second[...] = jnp.dot(hot2[n], results, preferred_element_type=f32).astype(bf16)
+        if n != 0:
+            remote(second, bt2.at[n], sbt.at[1], rbt.at[1], b_peer(boff)[1]).start()
 
     def merge(ref):
         merged = ref[0].astype(f32)
@@ -388,8 +397,8 @@
         vmem((8, 80, HD), bf16),
         vmem((8, 32, HD), bf16),
         vmem((8, 32, HD), bf16),
-        vmem((8, 128, 512), bf16),
-        vmem((128, 512), bf16),
+        vmem((8, 64, 512), bf16),
+        vmem((8, 80, 512), bf16),
         vmem((512, HD), bf16),
         vmem((128, HD), f32),
         vmem((128, HD), f32),

time: 50.3 us -> 49.4 us (0.982)
  Pallas kernels: 48.8 us -> 47.9 us
    pallas_call x1, Pallas kernels: 48.8 us -> 47.9 us  [shards(): pl.pallas_call(kernel, out_shape=jax.ShapeDtypeStruct(residual.shape, bf1...]
where the time goes in v3:
time: 49.4 us; the launch traced here: 49.3 us
  Pallas kernels  47.9 us (97%)
  local copies, waits for them, and re-layouts  1.39 us (3%)
    pallas_call x1, Pallas kernels, shards(): pl.pallas_call(kernel, out_shape=jax.ShapeDtypeStruct(residual.shape, bf1...  47.9 us
    unnamed x1, local copies, waits for them, and re-layouts  1.39 us

profile of v3, /device:TPU:1, one launch (start us, length us, event | category | flops | bytes accessed | tf_op | source)
XLA Modules:
  0.0 49.3 jit_solution(14099557491664092500)
XLA Ops:
  0.0 47.9 %shard_map.91 = bf16[16,1152]{1,0:T(8,128)(2,1)} custom-call(bf16[16,1024]{1,0:T(8,128)(2,1)} %q_hbm.1, bf16[1,2,1024,512]{3,2,1,0:T(8,128)(2,1)} %kv_hbm.1, bf16[16,2,32,512]{3,2,1,0:T(8,128)(2,1)} %suf_hbm.1, s32[16]{0:T(128)} %len_hbm.1, s32[64]{0:T(128)} %pre_hbm.1, s32[4,64]{1,0:T(4,128)} %bitcast.1, bf16[1024,4608]{1,0:T(8,128)(2,1)} %w_hbm.1, ...), custom_call_target="tpu_custom_call" | custom-call | flops 500000000 | bytes 13000000 | tf_op jit(solution)/shard_map/pallas_call | solution.py:420
  47.9 1.4 %copy.11 = bf16[16,1152]{1,0:T(8,128)(2,1)} copy(bf16[16,1152]{1,0:T(8,128)(2,1)} %shard_map.91) | data formatting | bytes 73728

commit v4 on v3

--- a/solution.py
+++ b/solution.py
@@ -35,9 +35,9 @@
     qh, kv, suf, w, gain, res, len_s, pre_s, sam_s, sam_v,
     own_p, pick_s,
     qall, csend, qc, rsend, rc, bsend1, bsend2, bt1, bt2, asend, fin,
-    hot1, hot2, lmask, suf_o, suf_l, psend, pr, sqs, sqr,
+    hot1, hot2, lmask, sxs, sx, psend, pr, sqs, sqr,
     lq, lkv, lsuf, lw, lsmall, lint,
-    sa, ra, sb, rb, sc, rcs, sct, rct, sbt, rbt, sat, rat, srs, rrs, ssq, rsq,
+    sa, ra, sb, rb, sc, rcs, sct, rct, sbt, rbt, sat, rat, srs, rrs, ssq, rsq, sw, rw, ssx, rsx,
 ):
     me = lax.axis_index("grp")
     tp = lax.axis_index("tp")
@@ -58,9 +58,13 @@
         yy = (yh + off[1]) % 2
         return xx * 2 + yy, (grp_of(xx, z, yy), tp)
 
-    def tp_peer(off):
-        yy, cc = (tp // 2 + off // 2) % 2, (tp % 2 + off % 2) % 2
-        return yy * 2 + cc, (me, yy * 2 + cc)
+    chip, core = tp // 2, tp % 2
+    sibling_tp = chip * 2 + (1 - core)
+    sibling = (me, sibling_tp)
+    across = (me, (1 - chip) * 2 + core)
+
+    def z_sibling(off):
+        return (grp_of(x, (z + off) % 8, yh), sibling_tp)
 
     def remote(src, dst, send, recv, device):
         return pltpu.make_async_remote_copy(
@@ -73,8 +77,10 @@
         pl.semaphore_signal(barrier, inc=1, device_id=z_peer(off)[1], device_id_type=MESH)
     for off in B_FAR:
         pl.semaphore_signal(barrier, inc=1, device_id=b_peer(off)[1], device_id_type=MESH)
-    for off in (2, 3, 1):
-        pl.semaphore_signal(barrier, inc=1, device_id=tp_peer(off)[1], device_id_type=MESH)
+    for off in Z_FAR:
+        pl.semaphore_signal(barrier, inc=1, device_id=z_sibling(off), device_id_type=MESH)
+    for device in (across, sibling):
+        pl.semaphore_signal(barrier, inc=1, device_id=device, device_id_type=MESH)
 
     ints = [
         pltpu.make_async_copy(pre_hbm, pre_s, lint.at[0]),
@@ -102,8 +108,12 @@
     ]
     for copy in small:
         copy.start()
-    for t in range(4):
-        pltpu.make_async_copy(w_hbm.at[:, pl.ds(t * COLS, COLS)], w.at[t], lw).start()
+
+    def quarter(q, of_core):
+        return w_hbm.at[:, pl.ds(pl.multiple_of((2 * q + of_core) * COLS, HD), COLS)]
+
+    for q in range(2):
+        pltpu.make_async_copy(quarter(q, core), w.at[0, q], lw).start()
 
     for copy in ints:
         copy.wait()
@@ -121,12 +131,15 @@
             pick_s[off * SLOTS + s] = sam_s[s, found[off] & 63]
 
     pltpu.make_async_copy(qh, qh, lq).wait()
-    pl.semaphore_wait(barrier, 17)
+    pl.semaphore_wait(barrier, 23)
 
     for off in Z_FAR:
         zz, device = z_peer(off)
         remote(qh.at[zz], qall.at[off], sa, ra.at[off], device).start()
     qall[0] = qh[z]
+
+    for q in range(2):
+        remote(quarter(q, 1 - core), w.at[1, q], sw, rw, sibling).start()
 
     for off in (0,) + Z_NEAR:
         block = qall.at[off]
@@ -135,6 +148,43 @@
         for boff in B_FAR:
             slot = (boff[0] * 2 + boff[1]) * 8 + off
             remote(block, qall.at[slot], sb, rb, b_peer(boff)[1]).start()
+    pltpu.make_async_copy(suf, suf, lsuf).wait()
+    col = lax.broadcasted_iota(i32, (32, 512), 1)
+    srow = lax.broadcasted_iota(i32, (32, 512), 0) & 15
+    col_sample = col >> 5
+    live_len = jnp.zeros((32, 512), i32)
+    for s in range(SAMP):
+        live_len = jnp.where(col_sample == s, len_s[s], live_len)
+    live = (col_sample == srow) & ((col & 31) < live_len)
+    lower = lax.broadcasted_iota(i32, (8, HD), 1) < 64
+    for k in range(KVHEADS):
+        query = qh[pl.ds(2 * k, 2)].reshape(32, HD)
+        scores = (
+            lax.dot_general(
+                query, suf[0, k].reshape(512, HD), (((1,), (1,)), ((), ())),
+                preferred_element_type=f32,
+            )
+            * SCORE_SCALE
+        )
+        top = jnp.max(jnp.where(live, scores, NEG), axis=1, keepdims=True)
+        weights = jnp.where(live, jnp.exp(jnp.where(live, scores - top, 0.0)), 0.0)
+        total = jnp.sum(weights, axis=1, keepdims=True)
+        out = (
+            jnp.dot(weights.astype(bf16), suf[1, k].reshape(512, HD), preferred_element_type=f32)
+            / total
+        )
+        logs = jnp.broadcast_to(top + jnp.log(total), (32, HD))
+        for h in range(2):
+            at = h * SAMP
+            sxs[2 * k + h, pl.ds(0, SAMP)] = out[at : at + SAMP]
+            sxs[2 * k + h, pl.ds(SAMP, 8)] = jnp.where(
+                lower, logs[at : at + 8], logs[at + 8 : at + 16]
+            )
+    for off in Z_FAR:
+        zz, device = z_peer(off)
+        remote(sxs.at[zz], sx.at[off], ssx, rsx, device).start()
+    sx[0] = sxs[z]
+
     others = qall.at[pl.ds(8, 56)]
     remote(others, others, sb, rb, (me, tp)).wait_recv()
 
@@ -228,33 +278,6 @@
                     rsend.at[off], rc.at[off], sct, rct, z_peer(-off)[1]
                 ).start()
 
-    pltpu.make_async_copy(suf, suf, lsuf).wait()
-    col = lax.broadcasted_iota(i32, (32, 512), 1)
-    srow = lax.broadcasted_iota(i32, (32, 512), 0) & 15
-    col_sample = col >> 5
-    live_len = jnp.zeros((32, 512), i32)
-    for s in range(SAMP):
-        live_len = jnp.where(col_sample == s, len_s[s], live_len)
-    live = (col_sample == srow) & ((col & 31) < live_len)
-    for k in range(KVHEADS):
-        query = qh[pl.ds(2 * k, 2)].reshape(32, HD)
-        scores = (
-            lax.dot_general(
-                query, suf[0, k].reshape(512, HD), (((1,), (1,)), ((), ())),
-                preferred_element_type=f32,
-            )
-            * SCORE_SCALE
-        )
-        top = jnp.max(jnp.where(live, scores, NEG), axis=1, keepdims=True)
-        weights = jnp.where(live, jnp.exp(jnp.where(live, scores - top, 0.0)), 0.0)
-        total = jnp.sum(weights, axis=1, keepdims=True)
-        out = (
-            jnp.dot(weights.astype(bf16), suf[1, k].reshape(512, HD), preferred_element_type=f32)
-            / total
-        )
-        suf_o[pl.ds(k * 32, 32)] = out
-        suf_l[pl.ds(k * 32, 32)] = jnp.broadcast_to(top + jnp.log(total), (32, HD))
-
     seven = rc.at[pl.ds(1, 7)]
     remote(seven, seven, sct, rct, (me, tp)).wait_recv()
     results = rc[:, pl.ds(0, 64)].reshape(512, HD)
@@ -285,86 +308,88 @@
         merged = ref[0].astype(f32)
         for n in range(1, 8):
             merged = merged + ref[n].astype(f32)
-        return merged.astype(bf16)
-
-    def give(off, block, logs):
-        ref = fin if off == 0 else asend
-        ref[off, pl.ds(0, SAMP)] = block
-        ref[off, pl.ds(SAMP, SAMP)] = logs
-        if off != 0:
+        return merged
+
+    def give(off, prefix_out):
+        prefix_log = jnp.sum(
+            jnp.where((tile_lane >> 3) == off, logs, 0.0), axis=1, keepdims=True
+        )
+        suffix = sx[(8 - off) % 8]
+        suffix_log = jnp.concatenate([suffix[SAMP:, :1], suffix[SAMP:, 64:65]], axis=0)
+        joint = jnp.maximum(prefix_log, suffix_log)
+        share_p = jnp.exp(prefix_log - joint)
+        share_s = jnp.exp(suffix_log - joint)
+        attended = (share_p * prefix_out + share_s * suffix[:SAMP]) / (share_p + share_s)
+        asend[off] = attended.astype(bf16)
+        if off == 0:
+            fin[0] = asend[0]
+            remote(asend.at[0], fin.at[8], sat, rat, sibling).start()
+        else:
             remote(asend.at[off], fin.at[off], sat, rat, z_peer(off)[1]).start()
-
+            remote(asend.at[off], fin.at[8 + off], sat, rat, z_sibling(off)).start()
+
+    seven = sx.at[pl.ds(1, 7)]
+    remote(seven, seven, ssx, rsx, (me, tp)).wait_recv()
     seven = bt1.at[pl.ds(1, 7)]
     remote(seven, seven, sbt.at[0], rbt.at[0], (me, tp)).wait_recv()
     merged = merge(bt1)
     logs = merged[48:]
     for at, off in enumerate(Z_FAR[:3]):
-        give(off, merged[at * SAMP : (at + 1) * SAMP], logs)
+        give(off, merged[at * SAMP : (at + 1) * SAMP])
     seven = bt2.at[pl.ds(1, 7)]
     remote(seven, seven, sbt.at[1], rbt.at[1], (me, tp)).wait_recv()
     merged = merge(bt2)
     for at, off in enumerate(Z_FAR[3:] + (0,)):
-        give(off, merged[at * SAMP : (at + 1) * SAMP], logs)
-    pltpu.make_async_copy(w, w, lw).wait()
-    seven = fin.at[pl.ds(1, 7)]
-    remote(seven, seven, sat, rat, (me, tp)).wait_recv()
-
-    come = [fin[(z - i) % 8] for i in range(HEADS)]
-    prefix_out = jnp.concatenate([block[:SAMP] for block in come], axis=0).astype(f32)
-    log_tile = jnp.concatenate([block[SAMP:] for block in come], axis=0).astype(f32)
-    all_lane = lax.broadcasted_iota(i32, (128, HD), 1)
-    all_row = lax.broadcasted_iota(i32, (128, HD), 0)
-    prefix_log = jnp.sum(
-        jnp.where((all_lane >> 3) == ((z - (all_row >> 4)) & 7), log_tile, 0.0),
-        axis=1, keepdims=True,
-    )
-    suffix_log = suf_l[...]
-    joint = jnp.maximum(prefix_log, suffix_log)
-    share_p = jnp.exp(prefix_log - joint)
-    share_s = jnp.exp(suffix_log - joint)
-    attended = (
-        (share_p * prefix_out + share_s * suf_o[...]) / (share_p + share_s)
-    ).astype(bf16)
-    attended = jnp.concatenate(
-        [attended[i * SAMP : (i + 1) * SAMP] for i in range(HEADS)], axis=1
-    )
-
-    for off in (2, 3, 1):
-        tt, device = tp_peer(off)
-        psend[off - 1] = jnp.dot(attended, w[tt], preferred_element_type=f32).astype(bf16)
-        remote(psend.at[off - 1], pr.at[off - 1], srs, rrs, device).start()
-    projected = jnp.dot(attended, w[tp], preferred_element_type=f32)
-    remote(psend, pr, srs, rrs, (me, tp)).wait_recv()
-    for off in range(3):
-        projected = projected + pr[off].astype(f32)
+        give(off, merged[at * SAMP : (at + 1) * SAMP])
+    pltpu.make_async_copy(w.at[0], w.at[0], lw).wait()
+    remote(w.at[0], w.at[1], sw, rw, sibling).wait_recv()
+    others = fin.at[pl.ds(0, 15)]
+    remote(others, others, sat, rat, (me, tp)).wait_recv()
+
+    attended = [
+        jnp.concatenate([fin[side * 8 + (z - i) % 8] for i in range(HEADS)], axis=1)
+        for side in range(2)
+    ]
+
+    def project(q):
+        return sum(
+            jnp.dot(attended[side], w[side, q], preferred_element_type=f32)
+            for side in range(2)
+        )
+
+    other_part = project(1 - chip)
+    psend[0] = other_part.astype(bf16)
+    remote(psend.at[0], pr.at[0], srs, rrs, across).start()
+    own_part = project(chip)
+    psend[1] = own_part.astype(bf16)
+    remote(psend.at[1], pr.at[1], srs, rrs, across).start()
+    for copy in small:
+        copy.wait()
+    remote(psend, pr, srs, rrs, across).wait_recv()
+    projected = own_part + pr[0].astype(f32)
+    twin = other_part + pr[1].astype(f32)
     squares = jnp.zeros((SAMP, HD), f32)
     for n in range(COLS // HD):
-        piece = projected[:, n * HD : (n + 1) * HD]
-        squares = squares + piece * piece
+        for whole in (projected, twin):
+            piece = whole[:, n * HD : (n + 1) * HD]
+            squares = squares + piece * piece
     sqs[...] = squares
-    for off in (2, 3, 1):
-        remote(sqs, sqr.at[off - 1], ssq.at[off - 1], rsq, tp_peer(off)[1]).start()
-    for copy in small:
-        copy.wait()
-    remote(sqr, sqr, ssq.at[0], rsq, (me, tp)).wait_recv()
-    for off in range(3):
-        squares = squares + sqr[off]
+    remote(sqs, sqr, ssq, rsq, sibling).start()
+    remote(sqs, sqr, ssq, rsq, sibling).wait_recv()
+    squares = squares + sqr[...]
     scale = lax.rsqrt(jnp.sum(squares, axis=1, keepdims=True) / D + NORM_EPS)
     o_ref[...] = (res[...].astype(f32) + projected * scale * gain[...].reshape(1, COLS)).astype(bf16)
 
-    seven = qall.at[pl.ds(0, 7)]
-    remote(seven, seven, sa, ra.at[0], (me, tp)).wait_send()
-    seven = qall.at[pl.ds(0, 56)]
-    remote(seven, seven, sb, rb, (me, tp)).wait_send()
-    for ref, send, recv in (
-        (csend, sc, rcs.at[0]), (rc, sct, rct), (bt1, sbt.at[0], rbt.at[0]),
-        (bt2, sbt.at[1], rbt.at[1]), (fin, sat, rat),
+    for ref, count, send, recv in (
+        (qall, 7, sa, ra.at[0]), (qall, 56, sb, rb), (csend, 7, sc, rcs.at[0]),
+        (rc, 7, sct, rct), (bt1, 7, sbt.at[0], rbt.at[0]), (bt2, 7, sbt.at[1], rbt.at[1]),
+        (sx, 7, ssx, rsx), (fin, 15, sat, rat),
     ):
-        seven = ref.at[pl.ds(0, 7)]
-        remote(seven, seven, send, recv, (me, tp)).wait_send()
-    remote(psend, pr, srs, rrs, (me, tp)).wait_send()
-    for off in range(3):
-        remote(sqs, sqr.at[off], ssq.at[off], rsq, (me, tp)).wait_send()
+        some = ref.at[pl.ds(0, count)]
+        remote(some, some, send, recv, (me, tp)).wait_send()
+    remote(w.at[0], w.at[1], sw, rw, sibling).wait_send()
+    remote(psend, pr, srs, rrs, across).wait_send()
+    remote(sqs, sqr, ssq, rsq, sibling).wait_send()
 
 
 def shards(
@@ -377,7 +402,7 @@
         vmem((HEADS, SAMP, HD), bf16),
         vmem((2, KVHEADS, PREFIX, HD), bf16),
         vmem((2, KVHEADS, SAMP, SUF, HD), bf16),
-        vmem((4, HEADS * HD, COLS), bf16),
+        vmem((2, 2, HEADS * HD, COLS), bf16),
         vmem((COLS,), f32),
         vmem((SAMP, COLS), bf16),
         pltpu.SMEM((SAMP,), i32),
@@ -395,17 +420,17 @@
         vmem((8, 80, HD), bf16),
         vmem((8, 64, HD), bf16),
         vmem((8, 80, HD), bf16),
-        vmem((8, 32, HD), bf16),
-        vmem((8, 32, HD), bf16),
+        vmem((8, SAMP, HD), bf16),
+        vmem((16, SAMP, HD), bf16),
         vmem((8, 64, 512), bf16),
         vmem((8, 80, 512), bf16),
         vmem((512, HD), bf16),
-        vmem((128, HD), f32),
-        vmem((128, HD), f32),
-        vmem((3, SAMP, COLS), bf16),
-        vmem((3, SAMP, COLS), bf16),
+        vmem((8, 24, HD), f32),
+        vmem((8, 24, HD), f32),
+        vmem((2, SAMP, COLS), bf16),
+        vmem((2, SAMP, COLS), bf16),
         vmem((SAMP, HD), f32),
-        vmem((3, SAMP, HD), f32),
+        vmem((SAMP, HD), f32),
         dma, dma, dma, dma, dma((2,)), dma((4,)),
         dma, dma((8,)),
         dma, dma,
@@ -414,7 +439,9 @@
         dma((2,)), dma((2,)),
         dma, dma,
         dma, dma,
-        dma((3,)), dma,
+        dma, dma,
+        dma, dma,
+        dma, dma,
     ]
     anywhere = pl.BlockSpec(memory_space=pl.ANY)
     return pl.pallas_call(

time: 49.4 us -> 48.2 us (0.976)
  Pallas kernels: 47.9 us -> 46.7 us
    pallas_call x1, Pallas kernels: 47.9 us -> 46.7 us  [shards(): pl.pallas_call(kernel, out_shape=jax.ShapeDtypeStruct(residual.shape, bf1...]
where the time goes in v4:
time: 48.2 us; the launch traced here: 48.1 us
  Pallas kernels  46.7 us (97%)
  local copies, waits for them, and re-layouts  1.39 us (3%)
    pallas_call x1, Pallas kernels, shards(): pl.pallas_call(kernel, out_shape=jax.ShapeDtypeStruct(residual.shape, bf1...  46.7 us
    unnamed x1, local copies, waits for them, and re-layouts  1.39 us

profile of v4, /device:TPU:1, one launch (start us, length us, event | category | flops | bytes accessed | tf_op | source)
XLA Modules:
  0.0 48.1 jit_solution(9742499688451546662)
XLA Ops:
  0.0 46.7 %shard_map.91 = bf16[16,1152]{1,0:T(8,128)(2,1)} custom-call(bf16[16,1024]{1,0:T(8,128)(2,1)} %q_hbm.1, bf16[1,2,1024,512]{3,2,1,0:T(8,128)(2,1)} %kv_hbm.1, bf16[16,2,32,512]{3,2,1,0:T(8,128)(2,1)} %suf_hbm.1, s32[16]{0:T(128)} %len_hbm.1, s32[64]{0:T(128)} %pre_hbm.1, s32[4,64]{1,0:T(4,128)} %bitcast.1, bf16[1024,4608]{1,0:T(8,128)(2,1)} %w_hbm.1, ...), custom_call_target="tpu_custom_call" | custom-call | flops 500000000 | bytes 13000000 | tf_op jit(solution)/shard_map/pallas_call | solution.py:447
  46.7 1.4 %copy.11 = bf16[16,1152]{1,0:T(8,128)(2,1)} copy(bf16[16,1152]{1,0:T(8,128)(2,1)} %shard_map.91) | data formatting | bytes 73728

commit v5 on v4

--- a/solution.py
+++ b/solution.py
@@ -351,18 +351,21 @@
         for side in range(2)
     ]
 
-    def project(q):
-        return sum(
-            jnp.dot(attended[side], w[side, q], preferred_element_type=f32)
-            for side in range(2)
-        )
-
-    other_part = project(1 - chip)
-    psend[0] = other_part.astype(bf16)
-    remote(psend.at[0], pr.at[0], srs, rrs, across).start()
-    own_part = project(chip)
-    psend[1] = own_part.astype(bf16)
-    remote(psend.at[1], pr.at[1], srs, rrs, across).start()
+    def project(q, slot):
+        parts = []
+        for start, stop in ((0, 512), (512, COLS)):
+            at = pl.ds(start, stop - start)
+            part = sum(
+                jnp.dot(attended[side], w[side, q, :, at], preferred_element_type=f32)
+                for side in range(2)
+            )
+            psend[slot, :, at] = part.astype(bf16)
+            remote(psend.at[slot, :, at], pr.at[slot, :, at], srs, rrs, across).start()
+            parts.append(part)
+        return jnp.concatenate(parts, axis=1)
+
+    other_part = project(1 - chip, 0)
+    own_part = project(chip, 1)
     for copy in small:
         copy.wait()
     remote(psend, pr, srs, rrs, across).wait_recv()
@@ -451,14 +454,19 @@
         out_specs=pl.BlockSpec(memory_space=pltpu.VMEM),
         scratch_shapes=scratch,
         compiler_params=pltpu.CompilerParams(
-            collective_id=0, has_side_effects=True, vmem_limit_bytes=63 * 1024 * 1024
+            collective_id=0, has_side_effects=True, vmem_limit_bytes=48 * 1024 * 1024
         ),
         cost_estimate=pl.CostEstimate(
             flops=500_000_000, bytes_accessed=13_000_000, transcendentals=600_000
         ),
     )(
-        queries, prefix_kv, suffix_kv, suffix_len, prefill_group, sampler_groups.T,
-        out_weight, norm_gain, residual,
+        *[
+            pltpu.with_memory_space_constraint(operand, pltpu.HBM)
+            for operand in (
+                queries, prefix_kv, suffix_kv, suffix_len, prefill_group, sampler_groups.T,
+                out_weight, norm_gain, residual,
+            )
+        ]
     )
 
 

time: 48.2 us -> 46.8 us (0.971)
  local copies, waits for them, and re-layouts: 1.39 us -> 0.62 us
  Pallas kernels: 46.7 us -> 46.1 us
    unnamed x1, local copies, waits for them, and re-layouts: 1.39 us -> 0.62 us
    pallas_call x1, Pallas kernels: 46.7 us -> 46.1 us  [shards(): pl.pallas_call(kernel, out_shape=jax.ShapeDtypeStruct(residual.shape, bf1...]
where the time goes in v5:
time: 46.8 us; the launch traced here: 46.7 us
  Pallas kernels  46.1 us (99%)
  local copies, waits for them, and re-layouts  0.62 us (1%)
    pallas_call x1, Pallas kernels, shards(): pl.pallas_call(kernel, out_shape=jax.ShapeDtypeStruct(residual.shape, bf1...  46.1 us

profile of v5, /device:TPU:1, one launch (start us, length us, event | category | flops | bytes accessed | tf_op | source)
XLA Modules:
  0.0 46.7 jit_solution(14793854227429774174)
XLA Ops:
  0.0 46.1 %shard_map.91 = bf16[16,1152]{1,0:T(8,128)(2,1)S(1)} custom-call(bf16[16,1024]{1,0:T(8,128)(2,1)} %q_hbm.1, bf16[1,2,1024,512]{3,2,1,0:T(8,128)(2,1)} %kv_hbm.1, bf16[16,2,32,512]{3,2,1,0:T(8,128)(2,1)} %suf_hbm.1, s32[16]{0:T(128)} %len_hbm.1, s32[64]{0:T(128)} %pre_hbm.1, s32[4,64]{1,0:T(4,128)} %bitcast.1, bf16[1024,4608]{1,0:T(8,128)(2,1)} %w_hbm.1, ...), custom_call_target="tpu_custom_call" | custom-call | flops 500000000 | bytes 13000000 | tf_op jit(solution)/shard_map/pallas_call | solution.py:450
  46.1 0.6 %copy.11 = bf16[16,1152]{1,0:T(8,128)(2,1)} copy(bf16[16,1152]{1,0:T(8,128)(2,1)S(1)} %shard_map.91) | data formatting | bytes 73728

commit v6 on v5

--- a/solution.py
+++ b/solution.py
@@ -33,7 +33,7 @@
     q_hbm, kv_hbm, suf_hbm, len_hbm, pre_hbm, sam_hbm, w_hbm, gain_hbm, res_hbm,
     o_ref,
     qh, kv, suf, w, gain, res, len_s, pre_s, sam_s, sam_v,
-    own_p, pick_s,
+    own_p, pick_s, slot_s,
     qall, csend, qc, rsend, rc, bsend1, bsend2, bt1, bt2, asend, fin,
     hot1, hot2, lmask, sxs, sx, psend, pr, sqs, sqr,
     lq, lkv, lsuf, lw, lsmall, lint,
@@ -128,7 +128,10 @@
     for off in range(8):
         own_p[off] = found[off]
         for s in range(SLOTS):
-            pick_s[off * SLOTS + s] = sam_s[s, found[off] & 63]
+            g = sam_s[s, found[off] & 63]
+            pick_s[off * SLOTS + s] = g
+            near = ((x - (g >> 4)) & 3) * 2 + ((yh - g) & 1)
+            slot_s[off * SLOTS + s] = near * 8 + ((z - (g >> 1)) & 7)
 
     pltpu.make_async_copy(qh, qh, lq).wait()
     pl.semaphore_wait(barrier, 23)
@@ -190,9 +193,7 @@
 
     for off in Z_FAR + (0,):
         for s in range(SLOTS):
-            g = pick_s[off * SLOTS + s]
-            slot = (((x - (g >> 4)) & 3) * 2 + ((yh - g) & 1)) * 8 + ((z - (g >> 1)) & 7)
-            block = qall[slot]
+            block = qall[slot_s[off * SLOTS + s]]
             if off == 0:
                 qc[0, pl.ds(s * SAMP, SAMP)] = block
             else:
@@ -237,10 +238,13 @@
     tile_lane = lax.broadcasted_iota(i32, (SAMP, HD), 1)
     for c in range(32):
         of_z = ((pick_s[c] >> 1) - z) & 7
-        keep = ((tile_lane >> 3) == of_z) & (((tile_lane & 7) >> 1) == c % SLOTS)
+        keep = ((tile_lane >> 4) == of_z) & (((tile_lane & 15) >> 2) == c % SLOTS)
         lmask[pl.ds(c * SAMP, SAMP)] = jnp.where(keep, 1.0, 0.0).astype(bf16)
 
     pltpu.make_async_copy(kv, kv, lkv).wait()
+
+    which_part = lax.broadcasted_iota(i32, (64, HD), 1) & 3
+    which_slot = (tile_lane & 15) >> 2
 
     def attend(off):
         k = z_peer(-off)[0] // 2
@@ -255,13 +259,15 @@
         total = jnp.sum(weights, axis=1, keepdims=True)
         out = jnp.dot(weights.astype(bf16), kv[1, k], preferred_element_type=f32) / total
         log_total = top + jnp.log(total)
-        high = log_total.astype(bf16).astype(f32)
-        low = log_total - high
-        tile = jnp.zeros((SAMP, HD), f32)
-        for s in range(SLOTS):
-            at = s * SAMP
-            tile = jnp.where((tile_lane & 7) == 2 * s, high[at : at + SAMP], tile)
-            tile = jnp.where((tile_lane & 7) == 2 * s + 1, low[at : at + SAMP], tile)
+        wide = jnp.broadcast_to(log_total, (64, HD))
+        high = wide.astype(bf16).astype(f32)
+        middle = (wide - high).astype(bf16).astype(f32)
+        low = wide - high - middle
+        rest = jnp.where(which_part == 1, middle, jnp.where(which_part == 2, low, 0.0))
+        parts = jnp.where(which_part == 0, high, rest)
+        tile = parts[:SAMP]
+        for s in range(1, SLOTS):
+            tile = jnp.where(which_slot == s, parts[s * SAMP : (s + 1) * SAMP], tile)
         return out.astype(bf16), tile.astype(bf16)
 
     for group in ((4,), (3, 5), (2, 6), (1, 7), (0,)):
@@ -312,7 +318,7 @@
 
     def give(off, prefix_out):
         prefix_log = jnp.sum(
-            jnp.where((tile_lane >> 3) == off, logs, 0.0), axis=1, keepdims=True
+            jnp.where((tile_lane >> 4) == off, logs, 0.0), axis=1, keepdims=True
         )
         suffix = sx[(8 - off) % 8]
         suffix_log = jnp.concatenate([suffix[SAMP:, :1], suffix[SAMP:, 64:65]], axis=0)
@@ -413,6 +419,7 @@
         pltpu.SMEM((SLOTS, PROMPTS), i32),
         vmem((SLOTS, PROMPTS), i32),
         pltpu.SMEM((8,), i32),
+        pltpu.SMEM((32,), i32),
         pltpu.SMEM((32,), i32),
         vmem((64, SAMP, HD), bf16),
         vmem((8, 64, HD), bf16),

time: 46.8 us -> 46.9 us (level)
  no operation moved by 1% of the time
where the time goes in v6:
time: 46.9 us; the launch traced here: 46.8 us
  Pallas kernels  46.2 us (99%)
  local copies, waits for them, and re-layouts  0.62 us (1%)
    pallas_call x1, Pallas kernels, shards(): pl.pallas_call(kernel, out_shape=jax.ShapeDtypeStruct(residual.shape, bf1...  46.2 us

profile of v6, /device:TPU:1, one launch (start us, length us, event | category | flops | bytes accessed | tf_op | source)
XLA Modules:
  0.0 46.8 jit_solution(2281729473716270437)
XLA Ops:
  0.0 46.2 %shard_map.91 = bf16[16,1152]{1,0:T(8,128)(2,1)S(1)} custom-call(bf16[16,1024]{1,0:T(8,128)(2,1)} %q_hbm.1, bf16[1,2,1024,512]{3,2,1,0:T(8,128)(2,1)} %kv_hbm.1, bf16[16,2,32,512]{3,2,1,0:T(8,128)(2,1)} %suf_hbm.1, s32[16]{0:T(128)} %len_hbm.1, s32[64]{0:T(128)} %pre_hbm.1, s32[4,64]{1,0:T(4,128)} %bitcast.1, bf16[1024,4608]{1,0:T(8,128)(2,1)} %w_hbm.1, ...), custom_call_target="tpu_custom_call" | custom-call | flops 500000000 | bytes 13000000 | tf_op jit(solution)/shard_map/pallas_call | solution.py:457
  46.2 0.6 %copy.11 = bf16[16,1152]{1,0:T(8,128)(2,1)} copy(bf16[16,1152]{1,0:T(8,128)(2,1)S(1)} %shard_map.91) | data formatting | bytes 73728

commit v7 on v5

--- a/solution.py
+++ b/solution.py
@@ -113,7 +113,7 @@
         return w_hbm.at[:, pl.ds(pl.multiple_of((2 * q + of_core) * COLS, HD), COLS)]
 
     for q in range(2):
-        pltpu.make_async_copy(quarter(q, core), w.at[0, q], lw).start()
+        pltpu.make_async_copy(quarter(q, core), w.at[q, 0], lw).start()
 
     for copy in ints:
         copy.wait()
@@ -139,7 +139,7 @@
     qall[0] = qh[z]
 
     for q in range(2):
-        remote(quarter(q, 1 - core), w.at[1, q], sw, rw, sibling).start()
+        remote(quarter(q, 1 - core), w.at[q, 1], sw, rw, sibling).start()
 
     for off in (0,) + Z_NEAR:
         block = qall.at[off]
@@ -346,21 +346,22 @@
     others = fin.at[pl.ds(0, 15)]
     remote(others, others, sat, rat, (me, tp)).wait_recv()
 
-    attended = [
-        jnp.concatenate([fin[side * 8 + (z - i) % 8] for i in range(HEADS)], axis=1)
-        for side in range(2)
-    ]
+    attended = jnp.concatenate(
+        [fin[side * 8 + (z - i) % 8] for side in range(2) for i in range(HEADS)], axis=1
+    )
 
     def project(q, slot):
         parts = []
         for start, stop in ((0, 512), (512, COLS)):
             at = pl.ds(start, stop - start)
-            part = sum(
-                jnp.dot(attended[side], w[side, q, :, at], preferred_element_type=f32)
-                for side in range(2)
+            part = jnp.dot(
+                attended, w[q, :, :, at].reshape(2 * HEADS * HD, stop - start),
+                preferred_element_type=f32,
             )
             psend[slot, :, at] = part.astype(bf16)
-            remote(psend.at[slot, :, at], pr.at[slot, :, at], srs, rrs, across).start()
+            remote(
+                psend.at[slot, :, at], pr.at[slot, :, at], srs, rrs.at[slot], across
+            ).start()
             parts.append(part)
         return jnp.concatenate(parts, axis=1)
 
@@ -368,14 +369,16 @@
     own_part = project(chip, 1)
     for copy in small:
         copy.wait()
-    remote(psend, pr, srs, rrs, across).wait_recv()
-    projected = own_part + pr[0].astype(f32)
-    twin = other_part + pr[1].astype(f32)
-    squares = jnp.zeros((SAMP, HD), f32)
-    for n in range(COLS // HD):
-        for whole in (projected, twin):
+    def finish(part, slot, squares):
+        remote(psend.at[slot], pr.at[slot], srs, rrs.at[slot], across).wait_recv()
+        whole = part + pr[slot].astype(f32)
+        for n in range(COLS // HD):
             piece = whole[:, n * HD : (n + 1) * HD]
             squares = squares + piece * piece
+        return whole, squares
+
+    projected, squares = finish(own_part, 0, jnp.zeros((SAMP, HD), f32))
+    _, squares = finish(other_part, 1, squares)
     sqs[...] = squares
     remote(sqs, sqr, ssq, rsq, sibling).start()
     remote(sqs, sqr, ssq, rsq, sibling).wait_recv()
@@ -391,7 +394,7 @@
         some = ref.at[pl.ds(0, count)]
         remote(some, some, send, recv, (me, tp)).wait_send()
     remote(w.at[0], w.at[1], sw, rw, sibling).wait_send()
-    remote(psend, pr, srs, rrs, across).wait_send()
+    remote(psend, pr, srs, rrs.at[0], across).wait_send()
     remote(sqs, sqr, ssq, rsq, sibling).wait_send()
 
 
@@ -441,7 +444,7 @@
         dma, dma,
         dma((2,)), dma((2,)),
         dma, dma,
-        dma, dma,
+        dma, dma((2,)),
         dma, dma,
         dma, dma,
         dma, dma,

time: 46.8 us -> 46.8 us (level)
  no operation moved by 1% of the time
where the time goes in v7:
time: 46.8 us; the launch traced here: 46.7 us
  Pallas kernels  46.1 us (99%)
  local copies, waits for them, and re-layouts  0.62 us (1%)
    pallas_call x1, Pallas kernels, shards(): pl.pallas_call(kernel, out_shape=jax.ShapeDtypeStruct(residual.shape, bf1...  46.1 us

profile of v7, /device:TPU:1, one launch (start us, length us, event | category | flops | bytes accessed | tf_op | source)
XLA Modules:
  0.0 46.7 jit_solution(693424692655256481)
XLA Ops:
  0.0 46.1 %shard_map.91 = bf16[16,1152]{1,0:T(8,128)(2,1)S(1)} custom-call(bf16[16,1024]{1,0:T(8,128)(2,1)} %q_hbm.1, bf16[1,2,1024,512]{3,2,1,0:T(8,128)(2,1)} %kv_hbm.1, bf16[16,2,32,512]{3,2,1,0:T(8,128)(2,1)} %suf_hbm.1, s32[16]{0:T(128)} %len_hbm.1, s32[64]{0:T(128)} %pre_hbm.1, s32[4,64]{1,0:T(4,128)} %bitcast.1, bf16[1024,4608]{1,0:T(8,128)(2,1)} %w_hbm.1, ...), custom_call_target="tpu_custom_call" | custom-call | flops 500000000 | bytes 13000000 | tf_op jit(solution)/shard_map/pallas_call | solution.py:453
  46.1 0.6 %copy.11 = bf16[16,1152]{1,0:T(8,128)(2,1)} copy(bf16[16,1152]{1,0:T(8,128)(2,1)S(1)} %shard_map.91) | data formatting | bytes 73728
